TPU v7x, 256 devices: a whole 4x4x8 slice. The times are simulated.
256 devices in a mesh: col: 16 (over x, y_lo, core), rep: 16 (over y_hi, z).
Axes of the slice: x: 4, y: 4 (y_hi: 2, y_lo: 2; y = y_hi * 2 + y_lo), z: 8, core: 2. Of those that a mesh axis runs over, the one named last changes fastest.
Arguments:
- features: bfloat16 [32768, 512], P(('col', 'rep')), may hold values from -24 to 24
- reorder: int32 [256, 128], P(('col', 'rep')), may hold values from 0 to 127, each once within a row
- weight: bfloat16 [512, 512], replicated, may hold values from -0.25 to 0.25
- adjacency: bfloat16 [16, 16, 16, 16, 128, 128], P('col', 'rep'), may hold values from 0 to 10, as said below
- tile_block: int32 [16, 16, 16, 16], P('col', 'rep'), may hold values from 0 to 15
- live_counts: int32 [16, 16, 16], P('col', 'rep'), may hold values from 8 to 16, as said below
- grad_out: bfloat16 [32768, 512], P(('col', 'rep')), may hold values from -6 to 6
Outputs:
- activated: bfloat16 [32768, 512], P(('col', 'rep'))
- weight_grad: float32 [512, 512], P(('col', 'rep'))
- feature_grad: bfloat16 [32768, 512], P(('col', 'rep'))
Inputs may be any that keep to these rules, and one draw needn't show every extreme that they name: `adjacency`: edge weights are nonnegative. `live_counts`: some triple has all 16 slots live in every draw.
All inputs are finite; a program needn't handle non-finite values.
Results may differ from a plain program's by a relative error of at most 0.006.
Values may be sent and summed in bfloat16 or wider, within the bound.
A program may use at most 64 MiB of HBM per device.

v0:
```python
import math

import jax
import jax.numpy as jnp
from jax import lax
from jax.sharding import PartitionSpec as P


def shifted(x, axis, by):
    devices = lax.axis_size(axis)
    return lax.ppermute(x, axis, [(i, (i + by) % devices) for i in range(devices)])


def on_device(features, reorder, weight, adjacency, tile_block, live_counts, grad_out):
    tile_len = features.shape[0]
    feat_width = features.shape[1]
    groups = lax.axis_size("col")
    copies = lax.axis_size("rep")
    own_group = lax.axis_index("col")
    local_tiles = adjacency[0, 0]
    local_block = tile_block[0, 0]
    local_count = live_counts[0, 0]
    slot_count = local_tiles.shape[1]
    live_mask = jnp.arange(slot_count, dtype=jnp.int32)[None, :] < local_count[:, None]
    reordered = jnp.take(features, reorder[0], axis=0)
    projected = jnp.dot(reordered, weight, preferred_element_type=jnp.float32).astype(jnp.bfloat16)
    panel_rows = lax.all_gather(projected, "rep", axis=0, tiled=True).reshape(
        copies, tile_len, feat_width
    )
    row_weight = jnp.sum(
        jnp.where(live_mask[:, :, None], jnp.sum(local_tiles, axis=3, dtype=jnp.float32), 0.0),
        axis=1,
    )

    def select_pair(owner_id):
        tile_set = lax.dynamic_index_in_dim(local_tiles, owner_id, 0, False)
        block_ids = lax.dynamic_index_in_dim(local_block, owner_id, 0, False)
        live_flags = lax.dynamic_index_in_dim(live_mask, owner_id, 0, False)
        live_total = lax.dynamic_index_in_dim(local_count, owner_id, 0, False)
        return (tile_set, block_ids, live_flags, live_total)

    def forward_term(owner_id):
        tile_set, block_ids, live_flags, live_total = select_pair(owner_id)
        gathered = jnp.take(panel_rows, block_ids, axis=0)
        gathered = jnp.where(live_flags[:, None, None], gathered, jnp.zeros((), jnp.bfloat16))
        result_rows = jnp.einsum(
            "tij,tjf->if", tile_set, gathered, preferred_element_type=jnp.float32
        )
        return result_rows

    def carry_step(turn_index, carried):
        sums_acc, degree_acc = carried
        owner_id = (own_group - turn_index) % groups
        sums_acc = sums_acc + forward_term(owner_id)
        degree_acc = degree_acc + lax.dynamic_index_in_dim(row_weight, owner_id, 0, False)
        return shifted((sums_acc, degree_acc), "col", 1)

    start_state = (
        jnp.zeros((tile_len, feat_width), jnp.float32),
        jnp.zeros((tile_len,), jnp.float32),
    )
    summed_rows, degree_part = lax.fori_loop(0, groups, carry_step, start_state)
    scale = lax.rsqrt(1.0 + degree_part)[:, None]
    pre_act = summed_rows * scale + projected.astype(jnp.float32)
    activated = jax.nn.silu(pre_act).astype(jnp.bfloat16)
    sigmoid_val = jax.nn.sigmoid(pre_act)
    pre_grad = grad_out.astype(jnp.float32) * sigmoid_val * (1.0 + pre_act * (1.0 - sigmoid_val))
    scaled_rows = (pre_grad * scale).astype(jnp.bfloat16)

    def add_slot(totals, one_tile, block_id, factor, src_rows):
        contrib = (
            jnp.einsum("ij,if->jf", one_tile, src_rows, preferred_element_type=jnp.float32) * factor
        )
        current = lax.dynamic_index_in_dim(totals, block_id, 0, False)
        return lax.dynamic_update_index_in_dim(totals, current + contrib, block_id, 0)

    def backward_add(totals, owner_id, src_rows):
        tile_set, block_ids, live_flags, live_total = select_pair(owner_id)
        for slot_index in range(slot_count):
            totals = add_slot(
                totals,
                tile_set[slot_index],
                block_ids[slot_index],
                live_flags[slot_index].astype(jnp.float32),
                src_rows,
            )
        return totals

    start_totals = jnp.zeros((copies, tile_len, feat_width), jnp.float32)

    def spread_step(turn_index, carried):
        totals, src_rows = carried
        totals = backward_add(totals, (own_group - turn_index) % groups, src_rows)
        return (totals, shifted(src_rows, "col", 1))

    totals, last_rows = lax.fori_loop(0, groups - 1, spread_step, (start_totals, scaled_rows))
    totals = backward_add(totals, (own_group - groups + 1) % groups, last_rows)
    column_part = lax.psum_scatter(
        totals.reshape(copies * tile_len, feat_width), "rep", scatter_dimension=0, tiled=True
    )
    back_rows = (column_part + pre_grad).astype(jnp.bfloat16)
    node_total = tile_len * groups * copies
    weight_grad = lax.psum_scatter(
        jnp.einsum("nf,ng->fg", reordered, back_rows, preferred_element_type=jnp.float32),
        ("col", "rep"),
        scatter_dimension=0,
        tiled=True,
    ) * (1.0 / math.sqrt(node_total))
    input_rows = jnp.einsum(
        "ng,fg->nf", back_rows, weight, preferred_element_type=jnp.float32
    ).astype(jnp.bfloat16)
    feature_grad = jnp.zeros_like(features).at[reorder[0]].set(input_rows)
    return (activated, weight_grad, feature_grad)


def solution(mesh):
    return jax.shard_map(
        on_device,
        mesh=mesh,
        in_specs=(
            P(("col", "rep"), None),
            P(("col", "rep"), None),
            P(),
            P("col", "rep", None, None, None, None),
            P("col", "rep", None, None),
            P("col", "rep", None),
            P(("col", "rep"), None),
        ),
        out_specs=(P(("col", "rep"), None), P(("col", "rep"), None), P(("col", "rep"), None)),
        check_vma=False,
    )
```

profile of v0, /device:TPU:1, one launch (start us, length us, event | category | flops | bytes accessed | tf_op | source)
XLA Modules:
  0.0 2128.7 jit_solution(7322465692128387977)
XLA Ops:
  54.6 5.6 convert_reduce_fusion
  60.4 36.9 %all-gather.2.cloned.1.call-done = bf16[2048,512]{1,0:T(8,128)(2,1)} async-done(((bf16[128,512]{1,0:T(8,128)(2,1)}), bf16[2048,512]{1,0:T(8,128)(2,1)}) %all-gather.2.cloned.1.call-update) | async-done | bytes 2097168 | tf_op jit(solution)/shard_map/all_gather | solution.py:27
  97.4 224.1 %while.34 = (s32[]{:T(128)}, f32[128,512]{1,0:T(8,128)S(1)}, f32[128]{0:T(128)S(1)}, s32[]{:T(128)}, bf16[16,16,128,128]{3,2,1,0:T(8,128)(2,1)}, /*index=5*/pred...) while((s32[]{:T(128)}, f32[128,512]{1,0:T(8,128)S(1)}, ...), condition=%wide.region_3.4_spmd, body=%wide.region_2.3_spmd.sunk | while | flops 270599456 | bytes 8397068 | solution.py:62
  98.9 2.3 gather_fusion
  101.2 2.3 fusion.237
  103.5 4.5 collective-permute-start
  108.0 3.5 collective-permute-done.1
  113.0 2.3 gather_fusion
  115.2 2.3 fusion.237
  117.5 2.4 collective-permute-start
  120.1 3.5 collective-permute-done.1
  125.0 2.3 gather_fusion
  127.3 2.3 fusion.237
  129.6 2.4 collective-permute-start
  133.0 4.1 collective-permute-done.1
  138.7 2.3 gather_fusion
  141.0 2.3 fusion.237
  144.1 1.8 collective-permute-start.1
  145.9 5.3 collective-permute-done.1
  152.9 2.3 gather_fusion
  155.2 2.3 fusion.237
  158.9 6.5 collective-permute-done.1
  167.0 2.3 gather_fusion
  169.3 2.3 fusion.237
  171.8 7.7 collective-permute-done.1
  181.2 2.3 gather_fusion
  183.5 2.3 fusion.237
  185.9 7.8 collective-permute-done.1
  195.4 2.3 gather_fusion
  197.6 2.3 fusion.237
  200.0 7.8 collective-permute-done.1
  209.5 2.3 gather_fusion
  211.8 2.3 fusion.237
  214.2 7.8 collective-permute-done.1
  223.7 2.3 gather_fusion
  226.0 2.3 fusion.237
  228.4 7.8 collective-permute-done.1
  237.9 2.3 gather_fusion
  240.1 2.3 fusion.237
  242.5 7.8 collective-permute-done.1
  252.0 2.3 gather_fusion
  254.3 2.3 fusion.237
  256.7 7.8 collective-permute-done.1
  266.2 2.3 gather_fusion
  268.5 2.3 fusion.237
  270.9 7.8 collective-permute-done.1
  280.4 2.3 gather_fusion
  282.6 2.3 fusion.237
  285.0 7.8 collective-permute-done.1
  294.5 2.3 gather_fusion
  296.8 2.3 fusion.237
  299.2 7.8 collective-permute-done.1
  308.7 2.3 gather_fusion
  311.0 2.3 fusion.237
  313.4 7.8 collective-permute-done.1
  322.3 2.5 broadcast_in_dim.319
  324.8 1293.0 %while.35 = (s32[]{:T(128)}, f32[16,128,512]{2,1,0:T(8,128)}, bf16[128,512]{1,0:T(8,128)(2,1)S(1)}, s32[]{:T(128)}, s32[16,16]{1,0:T(8,128)}, /*index=5*/bf16[16...) while((s32[]{:T(128)}, f32[16,128,512]{2,1,0:T(8,128)}, ...), condition=%wide.region_5.6_spmd, body=%wide.region_4.5_spmd.sunk | while | flops 270532608 | bytes 20195080 | solution.py:96
  1175.5 2.7 collective-permute-start.2
  1263.1 2.9 collective-permute-start.2
  1350.9 4.6 collective-permute-start.2
  1440.4 2.9 collective-permute-start.2
  1528.3 4.5 collective-permute-start.2
  1660.3 197.2 %reduce-scatter.2.cloned.1.call-done = f32[128,512]{1,0:T(8,128)} async-done(((f32[2048,512]{1,0:T(8,128)}), f32[128,512]{1,0:T(8,128)}) %reduce-scatter.2.cloned.1.call-update) | async-done | bytes 262160 | tf_op jit(solution)/shard_map/reduce_scatter | solution.py:98
  1862.0 258.9 %all-reduce.3.cloned.1.call-done = f32[512,512]{1,0:T(8,128)} async-done(((f32[512,512]{1,0:T(8,128)}), f32[512,512]{1,0:T(8,128)}) %all-reduce.3.cloned.1.call-update) | async-done | bytes 1048592
  (768 shorter events, 756.3 us)
Async XLA Ops:
  7.2 3.2 copy-start
  7.2 90.1 %all-gather.2.cloned.1.call-start = ((), (), s32[]{:S(2)}) async-start(), calls=%async_computation.1 | async-start | bytes 2228224 | tf_op jit(solution)/shard_map/all_gather | solution.py:27
  11.4 1846.2 %reduce-scatter.2.cloned.1.call-start = ((), (), s32[]{:S(2)}) async-start(), calls=%async_computation.2 | async-start | bytes 4456448 | tf_op jit(solution)/shard_map/reduce_scatter | solution.py:98
  97.3 224.1 %copy-start.1 = (bf16[128,512]{1,0:T(8,128)(2,1)S(1)}, bf16[128,512]{1,0:T(8,128)(2,1)}, u32[]{:S(2)}) copy-start(bf16[128,512]{1,0:T(8,128)(2,1)} %convolution_convert_fusion.1) | copy-start | bytes 393220
  97.4 224.1 %copy-start.2 = (bf16[128,512]{1,0:T(8,128)(2,1)S(1)}, bf16[128,512]{1,0:T(8,128)(2,1)}, u32[]{:S(2)}) copy-start(bf16[128,512]{1,0:T(8,128)(2,1)} %param.17) | copy-start | bytes 393220
  103.5 8.1 collective-permute-start
  107.9 3.6 collective-permute-start.1
  117.5 6.1 collective-permute-start
  120.0 3.6 collective-permute-start.1
  129.6 7.7 collective-permute-start
  132.0 5.0 collective-permute-start.1
  143.3 8.2 collective-permute-start
  144.1 7.1 collective-permute-start.1
  157.4 8.2 collective-permute-start
  157.4 7.9 collective-permute-start.1
  171.6 8.2 collective-permute-start
  171.6 7.9 collective-permute-start.1
  185.8 8.2 collective-permute-start
  185.8 7.9 collective-permute-start.1
  199.9 8.2 collective-permute-start
  199.9 7.9 collective-permute-start.1
  214.1 8.2 collective-permute-start
  214.1 7.9 collective-permute-start.1
  228.3 8.2 collective-permute-start
  228.3 7.9 collective-permute-start.1
  242.4 8.2 collective-permute-start
  242.4 7.9 collective-permute-start.1
  256.6 8.2 collective-permute-start
  256.6 7.9 collective-permute-start.1
  270.8 8.2 collective-permute-start
  270.8 7.9 collective-permute-start.1
  284.9 8.2 collective-permute-start
  284.9 7.9 collective-permute-start.1
  299.1 8.2 collective-permute-start
  299.1 7.9 collective-permute-start.1
  313.2 8.2 collective-permute-start
  313.3 7.9 collective-permute-start.1
  324.8 85.1 %collective-permute-start.2 = (bf16[128,512]{1,0:T(8,128)(2,1)S(1)}, bf16[128,512]{1,0:T(8,128)(2,1)S(1)}, u32[]{:S(2)}, u32[]{:S(2)}) collective-permute-start(bf16[128,512]{1,0:T(8,128)(2,1)S(1)} %copy.40), channel_id=1, source_target_pairs={{0,16},{16,32},{32,48},{48,64},{64,80},{80,96},{96,112},{112,128},... | collective-permute-start | bytes 393224 | tf_op jit(solution)/shard_map/while/body/eval_jaxpr/ppermute | solution.py:11
  409.9 85.0 %collective-permute-start.2 = (bf16[128,512]{1,0:T(8,128)(2,1)S(1)}, bf16[128,512]{1,0:T(8,128)(2,1)S(1)}, u32[]{:S(2)}, u32[]{:S(2)}) collective-permute-start(bf16[128,512]{1,0:T(8,128)(2,1)S(1)} %copy.40), channel_id=1, source_target_pairs={{0,16},{16,32},{32,48},{48,64},{64,80},{80,96},{96,112},{112,128},... | collective-permute-start | bytes 393224 | tf_op jit(solution)/shard_map/while/body/eval_jaxpr/ppermute | solution.py:11
  494.9 85.1 %collective-permute-start.2 = (bf16[128,512]{1,0:T(8,128)(2,1)S(1)}, bf16[128,512]{1,0:T(8,128)(2,1)S(1)}, u32[]{:S(2)}, u32[]{:S(2)}) collective-permute-start(bf16[128,512]{1,0:T(8,128)(2,1)S(1)} %copy.40), channel_id=1, source_target_pairs={{0,16},{16,32},{32,48},{48,64},{64,80},{80,96},{96,112},{112,128},... | collective-permute-start | bytes 393224 | tf_op jit(solution)/shard_map/while/body/eval_jaxpr/ppermute | solution.py:11
  580.0 85.1 %collective-permute-start.2 = (bf16[128,512]{1,0:T(8,128)(2,1)S(1)}, bf16[128,512]{1,0:T(8,128)(2,1)S(1)}, u32[]{:S(2)}, u32[]{:S(2)}) collective-permute-start(bf16[128,512]{1,0:T(8,128)(2,1)S(1)} %copy.40), channel_id=1, source_target_pairs={{0,16},{16,32},{32,48},{48,64},{64,80},{80,96},{96,112},{112,128},... | collective-permute-start | bytes 393224 | tf_op jit(solution)/shard_map/while/body/eval_jaxpr/ppermute | solution.py:11
  665.1 85.1 %collective-permute-start.2 = (bf16[128,512]{1,0:T(8,128)(2,1)S(1)}, bf16[128,512]{1,0:T(8,128)(2,1)S(1)}, u32[]{:S(2)}, u32[]{:S(2)}) collective-permute-start(bf16[128,512]{1,0:T(8,128)(2,1)S(1)} %copy.40), channel_id=1, source_target_pairs={{0,16},{16,32},{32,48},{48,64},{64,80},{80,96},{96,112},{112,128},... | collective-permute-start | bytes 393224 | tf_op jit(solution)/shard_map/while/body/eval_jaxpr/ppermute | solution.py:11
  750.2 85.1 %collective-permute-start.2 = (bf16[128,512]{1,0:T(8,128)(2,1)S(1)}, bf16[128,512]{1,0:T(8,128)(2,1)S(1)}, u32[]{:S(2)}, u32[]{:S(2)}) collective-permute-start(bf16[128,512]{1,0:T(8,128)(2,1)S(1)} %copy.40), channel_id=1, source_target_pairs={{0,16},{16,32},{32,48},{48,64},{64,80},{80,96},{96,112},{112,128},... | collective-permute-start | bytes 393224 | tf_op jit(solution)/shard_map/while/body/eval_jaxpr/ppermute | solution.py:11
  835.3 85.1 %collective-permute-start.2 = (bf16[128,512]{1,0:T(8,128)(2,1)S(1)}, bf16[128,512]{1,0:T(8,128)(2,1)S(1)}, u32[]{:S(2)}, u32[]{:S(2)}) collective-permute-start(bf16[128,512]{1,0:T(8,128)(2,1)S(1)} %copy.40), channel_id=1, source_target_pairs={{0,16},{16,32},{32,48},{48,64},{64,80},{80,96},{96,112},{112,128},... | collective-permute-start | bytes 393224 | tf_op jit(solution)/shard_map/while/body/eval_jaxpr/ppermute | solution.py:11
  920.4 85.1 %collective-permute-start.2 = (bf16[128,512]{1,0:T(8,128)(2,1)S(1)}, bf16[128,512]{1,0:T(8,128)(2,1)S(1)}, u32[]{:S(2)}, u32[]{:S(2)}) collective-permute-start(bf16[128,512]{1,0:T(8,128)(2,1)S(1)} %copy.40), channel_id=1, source_target_pairs={{0,16},{16,32},{32,48},{48,64},{64,80},{80,96},{96,112},{112,128},... | collective-permute-start | bytes 393224 | tf_op jit(solution)/shard_map/while/body/eval_jaxpr/ppermute | solution.py:11
  1005.4 85.0 %collective-permute-start.2 = (bf16[128,512]{1,0:T(8,128)(2,1)S(1)}, bf16[128,512]{1,0:T(8,128)(2,1)S(1)}, u32[]{:S(2)}, u32[]{:S(2)}) collective-permute-start(bf16[128,512]{1,0:T(8,128)(2,1)S(1)} %copy.40), channel_id=1, source_target_pairs={{0,16},{16,32},{32,48},{48,64},{64,80},{80,96},{96,112},{112,128},... | collective-permute-start | bytes 393224 | tf_op jit(solution)/shard_map/while/body/eval_jaxpr/ppermute | solution.py:11
  1090.4 85.0 %collective-permute-start.2 = (bf16[128,512]{1,0:T(8,128)(2,1)S(1)}, bf16[128,512]{1,0:T(8,128)(2,1)S(1)}, u32[]{:S(2)}, u32[]{:S(2)}) collective-permute-start(bf16[128,512]{1,0:T(8,128)(2,1)S(1)} %copy.40), channel_id=1, source_target_pairs={{0,16},{16,32},{32,48},{48,64},{64,80},{80,96},{96,112},{112,128},... | collective-permute-start | bytes 393224 | tf_op jit(solution)/shard_map/while/body/eval_jaxpr/ppermute | solution.py:11
  1175.5 87.6 %collective-permute-start.2 = (bf16[128,512]{1,0:T(8,128)(2,1)S(1)}, bf16[128,512]{1,0:T(8,128)(2,1)S(1)}, u32[]{:S(2)}, u32[]{:S(2)}) collective-permute-start(bf16[128,512]{1,0:T(8,128)(2,1)S(1)} %copy.40), channel_id=1, source_target_pairs={{0,16},{16,32},{32,48},{48,64},{64,80},{80,96},{96,112},{112,128},... | collective-permute-start | bytes 393224 | tf_op jit(solution)/shard_map/while/body/eval_jaxpr/ppermute | solution.py:11
  1263.1 87.8 %collective-permute-start.2 = (bf16[128,512]{1,0:T(8,128)(2,1)S(1)}, bf16[128,512]{1,0:T(8,128)(2,1)S(1)}, u32[]{:S(2)}, u32[]{:S(2)}) collective-permute-start(bf16[128,512]{1,0:T(8,128)(2,1)S(1)} %copy.40), channel_id=1, source_target_pairs={{0,16},{16,32},{32,48},{48,64},{64,80},{80,96},{96,112},{112,128},... | collective-permute-start | bytes 393224 | tf_op jit(solution)/shard_map/while/body/eval_jaxpr/ppermute | solution.py:11
  1350.9 89.5 %collective-permute-start.2 = (bf16[128,512]{1,0:T(8,128)(2,1)S(1)}, bf16[128,512]{1,0:T(8,128)(2,1)S(1)}, u32[]{:S(2)}, u32[]{:S(2)}) collective-permute-start(bf16[128,512]{1,0:T(8,128)(2,1)S(1)} %copy.40), channel_id=1, source_target_pairs={{0,16},{16,32},{32,48},{48,64},{64,80},{80,96},{96,112},{112,128},... | collective-permute-start | bytes 393224 | tf_op jit(solution)/shard_map/while/body/eval_jaxpr/ppermute | solution.py:11
  1440.4 87.8 %collective-permute-start.2 = (bf16[128,512]{1,0:T(8,128)(2,1)S(1)}, bf16[128,512]{1,0:T(8,128)(2,1)S(1)}, u32[]{:S(2)}, u32[]{:S(2)}) collective-permute-start(bf16[128,512]{1,0:T(8,128)(2,1)S(1)} %copy.40), channel_id=1, source_target_pairs={{0,16},{16,32},{32,48},{48,64},{64,80},{80,96},{96,112},{112,128},... | collective-permute-start | bytes 393224 | tf_op jit(solution)/shard_map/while/body/eval_jaxpr/ppermute | solution.py:11
  1528.3 89.5 %collective-permute-start.2 = (bf16[128,512]{1,0:T(8,128)(2,1)S(1)}, bf16[128,512]{1,0:T(8,128)(2,1)S(1)}, u32[]{:S(2)}, u32[]{:S(2)}) collective-permute-start(bf16[128,512]{1,0:T(8,128)(2,1)S(1)} %copy.40), channel_id=1, source_target_pairs={{0,16},{16,32},{32,48},{48,64},{64,80},{80,96},{96,112},{112,128},... | collective-permute-start | bytes 393224 | tf_op jit(solution)/shard_map/while/body/eval_jaxpr/ppermute | solution.py:11
  1660.3 460.6 %all-reduce.3.cloned.1.call-start = ((), (), s32[]{:S(2)}) async-start(), calls=%async_computation.3 | async-start | bytes 2097152
Sparse Core Ops, SparseCore 0:
  11.5 85.7 all-gather.1
  1660.4 197.1 reduce-scatter.1
  1863.9 256.9 all-reduce.2
where the time goes:
time: 2170 us; the launch traced here: 2130 us
  waiting for transfers between devices  606 us (28%)
  loops' own time  606 us (28%)
  matrix products  470 us (22%)
  local copies, waits for them, and re-layouts  325 us (15%)
  between operations  54.2 us (2%)
  starting transfers between devices  34.2 us (2%)
  other arithmetic  33.5 us (2%)
    another operation x1, loops' own time, on_device(): lax.fori_loop(0, groups - 1, spread_step, (start_totals, scaled_rows))  606 us
    dot_general x256, matrix products, add_slot(): jnp.einsum('ij,if->jf', one_tile, src_rows, preferred_element_type=jnp.fl...  431 us
    unnamed x4, waiting for transfers between devices  259 us
    dynamic_slice x256, local copies, waits for them, and re-layouts, add_slot(): current = lax.dynamic_index_in_dim(totals, block_id, 0, False)  248 us
    reduce_scatter x1, waiting for transfers between devices, on_device(): lax.psum_scatter(totals.reshape(copies * tile_len, feat_width), 'rep', sc...  197 us
    ppermute x47, waiting for transfers between devices, shifted(): lax.ppermute(x, axis, [(i, (i + by) % devices) for i in range(devices)])  112 us
  transfers between devices with their start and end apart: 50, of which 33 were waited for; matrix products, arithmetic and copies ran while one was open for 32% of the time, Pallas kernels for 0%

commit v1 on v0

v1 whole, which is shorter than its diff:
```python
import functools
import math

import jax
import jax.numpy as jnp
from jax import lax
from jax.experimental import pallas as pl
from jax.experimental.pallas import tpu as pltpu
from jax.sharding import PartitionSpec as P

F32, BF16 = jnp.float32, jnp.bfloat16


def dot(a, b):
    return jnp.dot(a, b, preferred_element_type=F32)


def slab_kernel(block_ref, count_ref, tiles_ref, slab_ref, degree_ref, acc):
    k = pl.program_id(0)
    acc[...] = jnp.zeros_like(acc)

    def add(t, sums):
        b = block_ref[k, t]
        tile = tiles_ref[t].astype(F32)
        acc[b] = acc[b] + tile
        return sums + tile

    sums = lax.fori_loop(0, count_ref[k], add, jnp.zeros(acc.shape[1:], F32))
    slab_ref[...] = acc[...].astype(BF16)
    degree_ref[...] = jnp.broadcast_to(
        jnp.sum(sums.T, axis=0, keepdims=True), degree_ref.shape
    )


def dense_slab(tile_block, live_counts, adjacency):
    _, _, rows, slots, tile, _ = adjacency.shape
    blocks = 16
    return pl.pallas_call(
        slab_kernel,
        grid_spec=pltpu.PrefetchScalarGridSpec(
            num_scalar_prefetch=2,
            grid=(rows,),
            in_specs=[
                pl.BlockSpec(
                    (None, None, None, slots, tile, tile),
                    lambda k, *_: (0, 0, k, 0, 0, 0),
                )
            ],
            out_specs=[
                pl.BlockSpec((blocks, tile, tile), lambda k, *_: (0, k, 0)),
                pl.BlockSpec((None, 8, tile), lambda k, *_: (k, 0, 0)),
            ],
            scratch_shapes=[pltpu.VMEM((blocks, tile, tile), F32)],
        ),
        out_shape=[
            jax.ShapeDtypeStruct((blocks, rows * tile, tile), BF16),
            jax.ShapeDtypeStruct((rows, 8, tile), F32),
        ],
    )(tile_block, live_counts, adjacency)


GATHER = ["y0"] + [
    d + n for d in "pm" for n in ("w1", "w2", "w3", "w4", "o3", "o4", "y1", "y2")
]
FORWARD = [f"c{j}" for j in range(8)] + ["a", "b+", "b-", "c+", "c-", "d", "e+", "e-"]
BACK = [f"c{j}" for j in range(8)] + ["x+", "x-", "y", "h+", "h-", "y2", "n+", "n-"]
REDUCE = GATHER
SETS = [("g", GATHER), ("f", FORWARD), ("b", BACK), ("r", REDUCE)]
INDEX = {s + n: i for i, (s, n) in enumerate((s, n) for s, names in SETS for n in names)}
N_SEMS = len(INDEX)
PLACES = [(2, 1), (1, 1), (3, 1), (2, 0), (1, 0), (3, 0), (0, 1), (0, 0)]


def layer_kernel(
    feat_ref, order_ref, w_ref, slab_hbm, degree_ref, grad_ref,
    act_ref, wgrad_ref, fgrad_ref,
    slab, panel, projected, acc, stage_f, land_f, rows_t, totals, totals_low,
    stage_r, land_r, half_r, wsend, wland, wown, wsend2, wland2,
    slab_sem, send_sem, recv_sem, wsend_sem, wrecv_sem,
):
    tile, width = feat_ref.shape
    c, r = lax.axis_index("col"), lax.axis_index("rep")
    x, yl, core = c // 4, (c // 2) % 2, c % 2
    yh, z = r // 8, r % 8

    def group(dx, dy, dc):
        return ((x + dx) % 4) * 4 + ((yl + dy) % 2) * 2 + (core + dc) % 2

    def block(p, d):
        return ((yh + p) % 2) * 8 + (z + d + 8) % 8

    up, down, over = (c, block(0, 1)), (c, block(0, -1)), (c, block(1, 0))
    right, left, beside = (group(1, 0, 0), r), (group(3, 0, 0), r), (group(0, 1, 0), r)
    partner = (group(0, 0, 1), r)

    slab_copy = pltpu.make_async_copy(slab_hbm, slab, slab_sem)
    slab_copy.start()

    barrier = pltpu.get_barrier_semaphore()
    for device in (up, down, over, right, left, beside, partner):
        pl.semaphore_signal(barrier, 1, device_id=device)

    place = (
        lax.broadcasted_iota(jnp.int32, (tile, tile), 0) == order_ref[...]
    ).astype(F32)
    own = block(0, 0)
    panel[own] = dot(place.T.astype(BF16), feat_ref[...]).astype(BF16)

    pl.semaphore_wait(barrier, 7)
    copies = {}

    def send(name, src, dst, device):
        i = INDEX[name]
        copy = pltpu.make_async_remote_copy(
            src, dst, send_sem.at[i], recv_sem.at[i], device_id=device
        )
        copy.start()
        copies[name] = copy

    def arrived(name):
        copies[name].wait_recv()

    def pass_on(name, p, d, device, half=None):
        ref = panel.at[block(p, d)]
        if half is not None:
            ref = ref.at[pl.ds(half * tile // 2, tile // 2)]
        send("g" + name, ref, ref, device)

    def consume(b1, b2, first=False):
        for b in (b1, b2):
            projected[b] = dot(panel[b], w_ref[...]).astype(BF16)
        pair = jnp.concatenate([projected[b1], projected[b2]], axis=0)

        @pl.loop(0, slab.shape[1] // 512)
        def _(i):
            rows = pl.ds(pl.multiple_of(i * 512, 512), 512)
            part = dot(jnp.concatenate([slab[b1, rows], slab[b2, rows]], axis=1), pair)
            acc[rows] = part if first else acc[rows] + part

    ways = (("p", -1, up, 0), ("m", 1, down, 1))
    for way, s, device, h in ways:
        pass_on(way + "w1", 0, 0, device)
    pass_on("y0", 0, 0, over)
    for way, s, device, h in ways:
        arrived("g" + way + "w1")
        pass_on(way + "w2", 0, s, device)
        pass_on(way + "y1", 0, s, over)
    arrived("gy0")
    slab_copy.wait()
    consume(own, block(1, 0), first=True)
    for way, s, device, h in ways:
        arrived("g" + way + "w2")
        pass_on(way + "w3", 0, 2 * s, device)
        pass_on(way + "y2", 0, 2 * s, over)
    consume(block(0, 1), block(0, -1))
    for way, s, device, h in ways:
        arrived("g" + way + "w3")
        pass_on(way + "w4", 0, 3 * s, device, h)
        arrived("g" + way + "y1")
    consume(block(0, 2), block(0, -2))
    consume(block(1, 1), block(1, -1))
    for way, s, device, h in ways:
        arrived("g" + way + "y2")
        pass_on(way + "o3", 1, 2 * s, device)
    consume(block(0, 3), block(0, -3))
    for way, s, device, h in ways:
        arrived("g" + way + "w4")
        arrived("g" + way + "o3")
        pass_on(way + "o4", 1, 3 * s, device, h)
    consume(block(1, 2), block(1, -2))
    consume(block(1, 3), block(1, -3))
    for way, s, device, h in ways:
        arrived("g" + way + "o4")
    consume(block(0, 4), block(1, 4))

    def mine(dx, dy, dc=0):
        k = group(dx, dy, dc)
        rows = acc[pl.ds(pl.multiple_of(k * tile, tile), tile)]
        return rows, degree_ref[k][0:1]

    def pack(slot, value):
        rows, degree = value
        high = degree.astype(BF16)
        low = (degree - high.astype(F32)).astype(BF16)
        stage_f[slot, 0:tile] = rows.astype(BF16)
        stage_f[slot, tile : tile + 16] = jnp.concatenate(
            [
                jnp.broadcast_to(part, (16, tile))
                for part in (high, low, jnp.zeros_like(high), jnp.zeros_like(high))
            ],
            axis=1,
        )

    def degree_in(slot):
        tail = land_f[slot, tile : tile + 16].astype(F32)
        return tail[0:1, 0:tile] + tail[0:1, tile : 2 * tile]

    def plus(value, slot):
        rows, degree = value
        return rows + land_f[slot, 0:tile].astype(F32), degree + degree_in(slot)

    def ship(name, slot, device, lo=0, hi=tile + 16):
        span = pl.ds(lo, hi - lo)
        i = FORWARD.index(name)
        send("f" + name, stage_f.at[slot, span], land_f.at[i, span], device)

    at = {name: i for i, name in enumerate(FORWARD)}
    for j, (dx, dy) in enumerate(PLACES):
        pack(j, mine(dx, dy, 1))
        ship(f"c{j}", j, partner)

    def both(dx, dy):
        j = PLACES.index((dx, dy))
        arrived(f"fc{j}")
        return plus(mine(dx, dy), j)

    half = tile // 2
    pack(at["a"], both(2, 1))
    ship("a", at["a"], beside)
    for s, dx, device in (("+", 1, right), ("-", 3, left)):
        pack(at["b" + s], both(dx, 1))
        ship("b" + s, at["b" + s], device)
    far = both(2, 0)
    arrived("fa")
    pack(at["c+"], plus(far, at["a"]))
    ship("c+", at["c+"], right, 0, half)
    ship("c-", at["c+"], left, half, tile + 16)
    near = both(0, 1)
    for s in "+-":
        arrived("fb" + s)
        near = plus(near, at["b" + s])
    pack(at["d"], near)
    ship("d", at["d"], beside)
    rows, degree = both(1, 0)
    arrived("fc+")
    top = rows[:half] + land_f[at["c+"], 0:half].astype(F32)
    pack(at["e+"], (jnp.concatenate([top, rows[half:]], axis=0), degree))
    ship("e+", at["e+"], right)
    rows, degree = both(3, 0)
    arrived("fc-")
    bottom = rows[half:] + land_f[at["c-"], half:tile].astype(F32)
    pack(
        at["e-"],
        (jnp.concatenate([rows[:half], bottom], axis=0), degree + degree_in(at["c-"])),
    )
    ship("e-", at["e-"], left)
    whole = both(0, 0)
    for name in ("d", "e+", "e-"):
        arrived("f" + name)
        whole = plus(whole, at[name])

    summed, degree = whole
    scale = lax.rsqrt(1.0 + jnp.broadcast_to(degree, (tile, tile)).T)
    scale = jnp.concatenate([scale] * (width // tile), axis=1)
    pre_act = summed * scale + projected[own].astype(F32)
    sigmoid = 1.0 / (1.0 + jnp.exp(-pre_act))
    pre_grad = grad_ref[...].astype(F32) * sigmoid * (1.0 + pre_act * (1.0 - sigmoid))
    pre_grad_t = pre_grad.T
    rows_t[c] = (pre_grad * scale).T.astype(BF16)

    def hand(name, dx, dy, device, part=None):
        ref = rows_t.at[group(dx, dy, 0)]
        if part is not None:
            ref = ref.at[pl.ds(part * width // 2, width // 2)]
        send("b" + name, ref, ref, device)

    def to_partner(dx, dy):
        hand(f"c{PLACES.index((dx, dy))}", dx, dy, partner)

    hand("x+", 0, 0, right)
    hand("x-", 0, 0, left)
    hand("y", 0, 0, beside)
    to_partner(0, 0)
    act_ref[...] = (pre_act * sigmoid).astype(BF16)
    arrived("bx+")
    hand("h+", 3, 0, right, 0)
    arrived("bx-")
    hand("h-", 1, 0, left, 1)
    arrived("by")
    hand("n+", 0, 1, right)
    hand("n-", 0, 1, left)
    for place_at in ((3, 0), (1, 0), (0, 1)):
        to_partner(*place_at)
    arrived("bh+")
    arrived("bh-")
    hand("y2", 2, 0, beside)
    to_partner(2, 0)
    arrived("bn+")
    to_partner(3, 1)
    arrived("bn-")
    to_partner(1, 1)
    arrived("by2")
    to_partner(2, 1)
    for j in range(8):
        arrived(f"bc{j}")

    def column_sums(b1, b2):
        left_side = jnp.concatenate([rows_t[k] for k in range(rows_t.shape[0])], axis=1)
        sums = dot(left_side, jnp.concatenate([slab[b1], slab[b2]], axis=1))
        for b, part in ((b1, sums[:, :tile]), (b2, sums[:, tile:])):
            totals[b] = part
            totals_low[b] = part.astype(BF16)

    where = {name: i for i, name in enumerate(REDUCE)}
    ways = (("m", -1, down, 0), ("p", 1, up, 1))
    middle = width // 2

    def leaf_half(way, kind, p, h, device):
        name = way + kind
        i = ("m", "p").index(way) * 2 + ("w4", "o4").index(kind)
        src = totals_low.at[block(p, 4), pl.ds(h * middle, middle)]
        send("r" + name, src, half_r.at[i], device)

    def leaf(name, p, d, device):
        send("r" + name, totals_low.at[block(p, d)], land_r.at[where[name]], device)

    def join_half(name, kind, p, d, way, h, device):
        arrived("r" + way + kind)
        i = ("m", "p").index(way) * 2 + ("w4", "o4").index(kind)
        b, slot = block(p, d), where[name]
        mid, rest = pl.ds(h * middle, middle), pl.ds((1 - h) * middle, middle)
        stage_r[slot, mid] = (totals[b, mid] + half_r[i].astype(F32)).astype(BF16)
        stage_r[slot, rest] = totals_low[b, rest]
        send("r" + name, stage_r.at[slot], land_r.at[slot], device)

    def join(name, children, p, d, device):
        value = totals[block(p, d)]
        for child in children:
            arrived("r" + child)
            value = value + land_r[where[child]].astype(F32)
        slot = where[name]
        stage_r[slot] = value.astype(BF16)
        send("r" + name, stage_r.at[slot], land_r.at[slot], device)

    column_sums(block(0, 4), block(1, 4))
    for way, s, device, h in ways:
        leaf_half(way, "o4", 1, h, device)
        leaf_half(way, "w4", 0, h, device)
    column_sums(block(1, 1), block(1, -1))
    for way, s, device, h in ways:
        leaf(way + "y1", 1, s, over)
    column_sums(block(1, 3), block(1, -3))
    for way, s, device, h in ways:
        join_half(way + "o3", "o4", 1, 3 * s, way, h, device)
    column_sums(block(0, 3), block(0, -3))
    for way, s, device, h in ways:
        join_half(way + "w3", "w4", 0, 3 * s, way, h, device)
    column_sums(block(1, 2), block(1, -2))
    for way, s, device, h in ways:
        join(way + "y2", [way + "o3"], 1, 2 * s, over)
    column_sums(block(1, 0), own)
    leaf("y0", 1, 0, over)
    column_sums(block(0, 2), block(0, -2))
    for way, s, device, h in ways:
        join(way + "w2", [way + "w3", way + "y2"], 0, 2 * s, device)
    column_sums(block(0, 1), block(0, -1))
    for way, s, device, h in ways:
        join(way + "w1", [way + "w2", way + "y1"], 0, s, device)

    blocks = range(panel.shape[0])
    slim = width // 16
    grad_low = pre_grad_t.astype(BF16)
    for i in range(width // tile):
        columns = slice(i * tile, (i + 1) * tile)
        term = dot(
            jnp.concatenate([totals_low[b] for b in blocks] + [grad_low], axis=1),
            jnp.concatenate(
                [panel[b, :, columns] for b in blocks] + [panel[own][:, columns]], axis=0
            ),
        ).T
        wown[columns] = term
        for j in range(tile // slim):
            wsend[i * (tile // slim) + j] = term[j * slim : (j + 1) * slim].astype(BF16)
    wcopies = []
    for i in range(1, 16):
        to = lax.rem(c + i, 16)
        copy = pltpu.make_async_remote_copy(
            wsend.at[to], wland.at[i], wsend_sem.at[i], wrecv_sem.at[i], device_id=(to, r)
        )
        copy.start()
        wcopies.append(copy)
    total = wown[pl.ds(pl.multiple_of(c * slim, slim), slim)]
    for i, copy in enumerate(wcopies):
        copy.wait_recv()
        total = total + wland[i + 1].astype(F32)
    two = slim // 16
    for i in range(16):
        wsend2[i, 0:two] = total[i * two : (i + 1) * two]
    wcopies2 = []
    for i in range(1, 16):
        to = lax.rem(r + i, 16)
        copy = pltpu.make_async_remote_copy(
            wsend2.at[to], wland2.at[i], wsend_sem.at[16 + i], wrecv_sem.at[16 + i],
            device_id=(c, to),
        )
        copy.start()
        wcopies2.append(copy)

    back_t = totals[own] + pre_grad_t
    for name in ("mw1", "pw1", "y0"):
        arrived("r" + name)
        back_t = back_t + land_r[where[name]].astype(F32)
    back = back_t.T.astype(BF16)
    input_rows = lax.dot_general(
        back, w_ref[...], (((1,), (1,)), ((), ())), preferred_element_type=F32
    ).astype(BF16)
    fgrad_ref[...] = dot(place.astype(BF16), input_rows).astype(BF16)

    pair = wsend2[r][0:two]
    for i, copy in enumerate(wcopies2):
        copy.wait_recv()
        pair = pair + wland2[i + 1][0:two]
    wgrad_ref[...] = pair * (1.0 / math.sqrt(tile * 256))
    for copy in [*copies.values(), *wcopies, *wcopies2]:
        copy.wait_send()


def on_device(features, reorder, weight, adjacency, tile_block, live_counts, grad_out):
    tile, width = features.shape
    slab, degree = dense_slab(tile_block[0, 0], live_counts[0, 0], adjacency)
    vmem = pl.BlockSpec(memory_space=pltpu.VMEM)
    rows = slab.shape[1]
    return pl.pallas_call(
        layer_kernel,
        in_specs=[vmem, vmem, vmem, pl.BlockSpec(memory_space=pl.ANY), vmem, vmem],
        out_specs=[vmem, vmem, vmem],
        out_shape=[
            jax.ShapeDtypeStruct((tile, width), BF16),
            jax.ShapeDtypeStruct((width // 256, width), F32),
            jax.ShapeDtypeStruct((tile, width), BF16),
        ],
        scratch_shapes=[
            pltpu.VMEM(slab.shape, BF16),
            pltpu.VMEM((16, tile, width), BF16),
            pltpu.VMEM((16, tile, width), BF16),
            pltpu.VMEM((rows, width), F32),
            pltpu.VMEM((len(FORWARD), tile + 16, width), BF16),
            pltpu.VMEM((len(FORWARD), tile + 16, width), BF16),
            pltpu.VMEM((16, width, tile), BF16),
            pltpu.VMEM((16, width, tile), F32),
            pltpu.VMEM((16, width, tile), BF16),
            pltpu.VMEM((len(REDUCE), width, tile), BF16),
            pltpu.VMEM((len(REDUCE), width, tile), BF16),
            pltpu.VMEM((4, width // 2, tile), BF16),
            pltpu.VMEM((16, width // 16, width), BF16),
            pltpu.VMEM((16, width // 16, width), BF16),
            pltpu.VMEM((width, width), F32),
            pltpu.VMEM((16, 8, width), F32),
            pltpu.VMEM((16, 8, width), F32),
            pltpu.SemaphoreType.DMA,
            pltpu.SemaphoreType.DMA((N_SEMS,)),
            pltpu.SemaphoreType.DMA((N_SEMS,)),
            pltpu.SemaphoreType.DMA((32,)),
            pltpu.SemaphoreType.DMA((32,)),
        ],
        compiler_params=pltpu.CompilerParams(
            collective_id=0, has_side_effects=True, vmem_limit_bytes=56 * 2**20
        ),
    )(features, reorder, weight, slab, degree, grad_out)


def solution(mesh):
    nodes = P(("col", "rep"), None)
    return jax.shard_map(
        on_device,
        mesh=mesh,
        in_specs=(
            nodes,
            nodes,
            P(),
            P("col", "rep", None, None, None, None),
            P("col", "rep", None, None),
            P("col", "rep", None),
            nodes,
        ),
        out_specs=(nodes, nodes, nodes),
        check_vma=False,
    )
```

time: 2170 us -> 133 us (0.06); the launches traced: 2130 us -> 133 us
  loops' own time: 606 us -> 0 us
  waiting for transfers between devices: 606 us -> 0 us
  matrix products: 470 us -> 0 us
  local copies, waits for them, and re-layouts: 325 us -> 4.4 us
  Pallas kernels: 0 us -> 128 us
  between operations: 54.2 us -> 0.64 us
  starting transfers between devices: 34.2 us -> 0 us
  other arithmetic: 33.5 us -> 0 us
    another operation x2 -> x0, loops' own time: 606 us -> none  [the longest x1 606 us: on_device(): lax.fori_loop(0, groups - 1, spread_step, (start_totals, scaled_rows))]
    dot_general x275 -> x0, matrix products: 470 us -> none  [the longest x256 431 us: add_slot(): jnp.einsum('ij,if->jf', one_tile, src_rows, preferred_element_type=jnp.fl...]
    dynamic_slice x288 -> x0, local copies, waits for them, and re-layouts: 259 us -> none  [the longest x256 248 us: add_slot(): current = lax.dynamic_index_in_dim(totals, block_id, 0, False)]
    unnamed x4 -> x0, waiting for transfers between devices: 259 us -> none
    reduce_scatter x1 -> x0, waiting for transfers between devices: 197 us -> none  [on_device(): lax.psum_scatter(totals.reshape(copies * tile_len, feat_width), 'rep', sc...]
    pallas_call x0 -> x2, Pallas kernels: none -> 128 us  [the longest x1 113 us: on_device(): pl.pallas_call(layer_kernel, in_specs=[vmem, vmem, vmem, pl.BlockSpec(mem...]
    ppermute x47 -> x0, waiting for transfers between devices: 112 us -> none  [shifted(): lax.ppermute(x, axis, [(i, (i + by) % devices) for i in range(devices)])]
    gather x17 -> x0, local copies, waits for them, and re-layouts: 38.2 us -> none  [the longest x16 36.4 us: forward_term(): gathered = jnp.take(panel_rows, block_ids, axis=0)]
  transfers between devices with their start and end apart: 50 -> 0, of which waited for: 33 -> 0; matrix products, arithmetic and copies ran while one was open for 32% -> 0% of each run, Pallas kernels for 0% -> 0%
where the time goes in v1:
time: 133 us
  Pallas kernels  128 us (96%)
  local copies, waits for them, and re-layouts  4.4 us (3%)
    pallas_call x1, Pallas kernels, on_device(): pl.pallas_call(layer_kernel, in_specs=[vmem, vmem, vmem, pl.BlockSpec(mem...  113 us
    pallas_call x1, Pallas kernels, dense_slab(): pl.pallas_call(slab_kernel, grid_spec=pltpu.PrefetchScalarGridSpec(num_sc...  14.5 us
    unnamed x3, local copies, waits for them, and re-layouts  4.4 us

profile of v1, /device:TPU:1, one launch (start us, length us, event | category | flops | bytes accessed | tf_op | source)
XLA Modules:
  0.0 132.6 jit_solution(16357698474400751820)
XLA Ops:
  0.6 14.5 %shard_map.94 = (bf16[16,2048,128]{2,1,0:T(8,128)(2,1)}, f32[16,8,128]{2,1,0:T(8,128)}) custom-call(s32[16,16]{1,0:T(8,128)} %bitcast.2, s32[16]{0:T(128)} %bitcast.3, bf16[1,1,16,16,128,128]{5,4,3,2,1,0:T(8,128)(2,1)} %tiles_ref.1), custom_call_target="tpu_custom_call" | custom-call | tf_op jit(solution)/shard_map/pallas_call | solution.py:38
  15.2 113.1 %shard_map.95 = (bf16[128,512]{1,0:T(8,128)(2,1)}, f32[2,512]{1,0:T(2,128)}, bf16[128,512]{1,0:T(8,128)(2,1)}) custom-call(bf16[128,512]{1,0:T(8,128)(2,1)} %feat_ref.1, s32[1,128]{1,0:T(1,128)} %order_ref.1, bf16[512,512]{1,0:T(8,128)(2,1)} %w_ref.1, bf16[16,2048,128]{2,1,0:T(8,128)(2,1)} %get-tuple-element.5.slab_hbm, ...), custom_call_target="tpu_custom_call" | custom-call | tf_op jit(solution)/shard_map/pallas_call | solution.py:423
  128.2 1.6 %copy.13 = bf16[128,512]{1,0:T(8,128)(2,1)} copy(bf16[128,512]{1,0:T(8,128)(2,1)} %get-tuple-element.10) | data formatting | bytes 262144
  129.8 1.3 copy.14
  131.1 1.6 %copy.15 = bf16[128,512]{1,0:T(8,128)(2,1)} copy(bf16[128,512]{1,0:T(8,128)(2,1)} %get-tuple-element.12) | data formatting | bytes 262144

commit v2 on v1

v2 whole, which is shorter than its diff:
```python
import math

import jax
import jax.numpy as jnp
from jax import lax
from jax.experimental import pallas as pl
from jax.experimental.pallas import tpu as pltpu
from jax.sharding import PartitionSpec as P

F32, BF16 = jnp.float32, jnp.bfloat16


def dot(a, b):
    return jnp.dot(a, b, preferred_element_type=F32)


OVER_REP = ["y00", "y01"] + [
    d + n
    for d in "pm"
    for n in ("w10", "w11", "w20", "w21", "w30", "w31", "w4", "o20", "o21", "o30", "o31", "o4", "y10", "y11")
]
FORWARD = [f"c{j}" for j in range(8)] + [
    n for m in ("a", "b+", "b-", "k", "d", "e+", "e-") for n in (m + "0", m + "1")
]
BACK = [f"c{j}" for j in range(8)] + [
    n for m in ("x+", "x-", "y", "h", "t", "n+", "n-") for n in (m + "0", m + "1")
]
SETS = [("g", OVER_REP), ("f", FORWARD), ("b", BACK), ("r", OVER_REP)]
INDEX = {n: i for i, n in enumerate(s + n for s, names in SETS for n in names)}
N_SEMS = len(INDEX)
SLOTS = {n: i for i, n in enumerate([f"c{j}" for j in range(8)] + ["a", "b+", "b-", "k", "d", "e+", "e-"])}
PIECES = {n: i for i, n in enumerate(["y0"] + [d + n for d in "pm" for n in ("w1", "w2", "w3", "w4", "o2", "o3", "o4", "y1")])}
PLACES = [(2, 1), (1, 1), (3, 1), (1, 0), (3, 0), (2, 0), (0, 1), (0, 0)]


def layer_kernel(
    feat_ref, order_ref, w_ref, tiles_hbm, block_ref, count_ref, grad_ref,
    act_ref, wgrad_ref, fgrad_ref,
    tiles, slab, ids, degrees, panel, projected, acc, stage_f, land_f, rows_t, totals, totals_low,
    stage_r, land_r, wsend, wland, wown, wsend2, wland2,
    tile_sem, send_sem, recv_sem, wsend_sem, wrecv_sem,
):
    tile, width = feat_ref.shape
    n_rows, n_slots = tiles.shape[:2]
    c, r = lax.axis_index("col"), lax.axis_index("rep")
    x, yl, core = c // 4, (c // 2) % 2, c % 2
    yh, z = r // 8, r % 8

    def group(dx, dy, dc):
        return ((x + dx) % 4) * 4 + ((yl + dy) % 2) * 2 + (core + dc) % 2

    def block(p, d):
        return ((yh + p) % 2) * 8 + (z + d + 8) % 8

    up, down, over = (c, block(0, 1)), (c, block(0, -1)), (c, block(1, 0))
    right, left, beside = (group(1, 0, 0), r), (group(3, 0, 0), r), (group(0, 1, 0), r)
    partner = (group(0, 0, 1), r)

    def fetch(k):
        return pltpu.make_async_copy(tiles_hbm.at[0, 0, k], tiles.at[k], tile_sem.at[k])

    barrier = pltpu.get_barrier_semaphore()
    for device in (up, down, over, right, left, beside, partner):
        pl.semaphore_signal(barrier, 1, device_id=device)

    @pl.loop(0, n_rows)
    def _(k):
        fetch(k).start()

    def iota(shape, dim):
        return lax.broadcasted_iota(jnp.int32, shape, dim)

    place = (iota((tile, tile), 0) == order_ref[...]).astype(F32)
    own = block(0, 0)
    panel[own] = dot(place.T.astype(BF16), feat_ref[...]).astype(BF16)

    n_blocks, strip = slab.shape[0], 16
    wide = n_slots * strip
    spread = (iota((n_slots, wide), 1) // strip == iota((n_slots, wide), 0)).astype(BF16)
    ids[...] = dot(block_ref[0, 0].astype(F32).astype(BF16), spread)

    def build(k):
        fetch(k).wait()
        shape = (n_blocks * strip + strip, wide)
        out_at, in_at = iota(shape, 0), iota(shape, 1)
        picked = (ids[pl.ds(k, 1), :] == (out_at // strip).astype(F32)) | (out_at >= n_blocks * strip)
        live = in_at // strip < count_ref[0, 0, k]
        pick = picked & live & (out_at % strip == in_at % strip)
        pick = jnp.where(pick, 1.0, 0.0).astype(BF16)
        slots = jnp.concatenate(
            [tiles[k, :, g * strip : (g + 1) * strip, :].reshape(wide, tile) for g in range(tile // strip)],
            axis=1,
        )
        out = dot(pick, slots)

        def rows_of(b):
            part = out[b * strip : (b + 1) * strip]
            return jnp.concatenate(
                [part[:, g * tile : (g + 1) * tile] for g in range(tile // strip)], axis=0
            )

        rows = pl.ds(pl.multiple_of(k * tile, tile), tile)
        for b in range(n_blocks):
            slab[b, rows] = rows_of(b).astype(BF16)
        degrees[k] = jnp.broadcast_to(
            jnp.sum(rows_of(n_blocks).T, axis=0, keepdims=True), degrees.shape[1:]
        )

    pl.loop(0, n_rows // 2)(build)
    pl.semaphore_wait(barrier, 7)
    copies = {}

    def send(name, src, dst, device):
        i = INDEX[name]
        copy = pltpu.make_async_remote_copy(
            src, dst, send_sem.at[i], recv_sem.at[i], device_id=device
        )
        copy.start()
        copies[name] = copy

    def arrived(name):
        copies[name].wait_recv()

    half = tile // 2

    def pass_on(name, p, d, device, h):
        ref = panel.at[block(p, d), pl.ds(h * half, half)]
        send("g" + name, ref, ref, device)

    def consume(b1, b2, first=False):
        for b in (b1, b2):
            projected[b] = dot(panel[b], w_ref[...]).astype(BF16)
        pair = jnp.concatenate([projected[b1], projected[b2]], axis=0)

        @pl.loop(0, slab.shape[1] // 512)
        def _(i):
            rows = pl.ds(pl.multiple_of(i * 512, 512), 512)
            part = dot(jnp.concatenate([slab[b1, rows], slab[b2, rows]], axis=1), pair)
            acc[rows] = part if first else acc[rows] + part

    ways = (("p", -1, up, 0), ("m", 1, down, 1))
    for h in (0, 1):
        for way, s, device, _ in ways:
            pass_on(f"{way}w1{h}", 0, 0, device, h)
        pass_on(f"y0{h}", 0, 0, over, h)
    pl.loop(n_rows // 2, n_rows)(build)
    for h in (0, 1):
        for way, s, device, _ in ways:
            arrived(f"g{way}w1{h}")
            pass_on(f"{way}w2{h}", 0, s, device, h)
            pass_on(f"{way}y1{h}", 0, s, over, h)
    for h in (0, 1):
        arrived(f"gy0{h}")
    consume(own, block(1, 0), first=True)
    for h in (0, 1):
        for way, s, device, _ in ways:
            arrived(f"g{way}w2{h}")
            pass_on(f"{way}w3{h}", 0, 2 * s, device, h)
    consume(block(0, 1), block(0, -1))
    for h in (0, 1):
        for way, s, device, _ in ways:
            arrived(f"g{way}y1{h}")
            pass_on(f"{way}o2{h}", 1, s, device, h)
    consume(block(0, 2), block(0, -2))
    for way, s, device, e in ways:
        arrived(f"g{way}w3{e}")
        pass_on(f"{way}w4", 0, 3 * s, device, e)
    consume(block(1, 1), block(1, -1))
    for h in (0, 1):
        for way, s, device, e in ways:
            arrived(f"g{way}o2{(h + e) % 2}")
            pass_on(f"{way}o3{(h + e) % 2}", 1, 2 * s, device, (h + e) % 2)
    for way, s, device, e in ways:
        arrived(f"g{way}w3{1 - e}")
    consume(block(0, 3), block(0, -3))
    for way, s, device, e in ways:
        arrived(f"g{way}o3{e}")
        pass_on(f"{way}o4", 1, 3 * s, device, e)
    consume(block(1, 2), block(1, -2))
    for way, s, device, e in ways:
        arrived(f"g{way}o3{1 - e}")
        arrived(f"g{way}w4")
    consume(block(1, 3), block(1, -3))
    for way, s, device, e in ways:
        arrived(f"g{way}o4")
    consume(block(0, 4), block(1, 4))

    def span(h):
        return slice(h * half, tile + 16 * h if h else half)

    def mine(dx, dy, dc, h):
        k = group(dx, dy, dc)
        rows = acc[pl.ds(pl.multiple_of(k * tile + h * half, half), half)]
        return rows, degrees[k][0:1]

    def pack(name, h, value):
        slot, (rows, degree) = SLOTS[name], value
        stage_f[slot, h * half : (h + 1) * half] = rows.astype(BF16)
        if h:
            high = degree.astype(BF16)
            low = (degree - high.astype(F32)).astype(BF16)
            none = jnp.zeros_like(high)
            stage_f[slot, tile : tile + 16] = jnp.concatenate(
                [jnp.broadcast_to(part, (16, tile)) for part in (high, low, none, none)], axis=1
            )

    def plus(value, name, h):
        slot, (rows, degree) = SLOTS[name], value
        rows = rows + land_f[slot, h * half : (h + 1) * half].astype(F32)
        if h:
            tail = land_f[slot, tile : tile + 16].astype(F32)
            degree = degree + tail[0:1, 0:tile] + tail[0:1, tile : 2 * tile]
        return rows, degree

    def ship(name, h, device):
        slot = SLOTS[name]
        at = pl.ds(span(h).start, span(h).stop - span(h).start)
        send(f"f{name}{h}", stage_f.at[slot, at], land_f.at[slot, at], device)

    for j, (dx, dy) in enumerate(PLACES):
        for h in (0, 1):
            pack(f"c{j}", h, mine(dx, dy, 1, h))
        send(f"fc{j}", stage_f.at[j], land_f.at[j], partner)

    def both(dx, dy, h):
        return plus(mine(dx, dy, 0, h), f"c{PLACES.index((dx, dy))}", h)

    def go(name, h, value, device):
        pack(name, h, value)
        ship(name, h, device)

    sides = (("+", 1, right, 0), ("-", 3, left, 1))
    arrived("fc0")
    for h in (0, 1):
        go("a", h, both(2, 1, h), beside)
    for j, (s, dx, device, e) in enumerate(sides):
        arrived(f"fc{1 + j}")
        go("b" + s, e, both(dx, 1, e), device)
        go("b" + s, 1 - e, both(dx, 1, 1 - e), device)
    for j, (s, dx, device, e) in enumerate(sides):
        arrived(f"fc{3 + j}")
        go("e" + s, 1 - e, both(dx, 0, 1 - e), device)
    arrived("fc5")
    for s, dx, device, e in sides:
        arrived(f"fa{e}")
        go("k", e, plus(both(2, 0, e), "a", e), device)
    arrived("fc6")
    for h in (0, 1):
        arrived(f"fb+{h}")
        arrived(f"fb-{h}")
        go("d", h, plus(plus(both(0, 1, h), "b+", h), "b-", h), beside)
    for s, dx, device, e in sides:
        arrived(f"fk{e}")
        go("e" + s, e, plus(both(dx, 0, e), "k", e), device)
    arrived("fc7")
    parts = []
    for h in (0, 1):
        value = both(0, 0, h)
        for name in ("d", "e+", "e-"):
            arrived(f"f{name}{h}")
            value = plus(value, name, h)
        parts.append(value)
    summed = jnp.concatenate([parts[0][0], parts[1][0]], axis=0)
    degree = parts[1][1]

    scale = lax.rsqrt(1.0 + jnp.broadcast_to(degree, (tile, tile)).T)
    scale = jnp.concatenate([scale] * (width // tile), axis=1)
    pre_act = summed * scale + projected[own].astype(F32)
    sigmoid = 1.0 / (1.0 + jnp.exp(-pre_act))
    pre_grad = grad_ref[...].astype(F32) * sigmoid * (1.0 + pre_act * (1.0 - sigmoid))
    rows_t[c] = (pre_grad * scale).T.astype(BF16)

    middle = width // 2

    def hand(name, dx, dy, device, h):
        ref = rows_t.at[group(dx, dy, 0), pl.ds(h * middle, middle)]
        send("b" + name, ref, ref, device)

    def to_partner(dx, dy):
        ref = rows_t.at[group(dx, dy, 0)]
        send(f"bc{PLACES.index((dx, dy))}", ref, ref, partner)

    for h in (0, 1):
        for s, dx, device, e in sides:
            hand(f"x{s}{(h + e) % 2}", 0, 0, device, (h + e) % 2)
        hand(f"y{h}", 0, 0, beside, h)
    to_partner(0, 0)
    pre_grad_t = pre_grad.T
    act_ref[...] = (pre_act * sigmoid).astype(BF16)
    for s, dx, device, e in sides:
        arrived(f"bx{s}{e}")
        hand(f"h{e}", 4 - dx, 0, device, e)
    for h in (0, 1):
        arrived(f"by{h}")
        for s, dx, device, e in sides:
            hand(f"n{s}{h}", 0, 1, device, h)
    for s, dx, device, e in sides:
        arrived(f"bx{s}{1 - e}")
        to_partner(4 - dx, 0)
    to_partner(0, 1)
    for e in (0, 1):
        arrived(f"bh{e}")
        hand(f"t{e}", 2, 0, beside, e)
    to_partner(2, 0)
    for s, dx, device, e in sides:
        arrived(f"bn{s}0")
        arrived(f"bn{s}1")
        to_partner(4 - dx, 1)
    arrived("bt0")
    arrived("bt1")
    to_partner(2, 1)
    for j in range(8):
        arrived(f"bc{j}")

    def column_sums(b1, b2):
        left_side = jnp.concatenate([rows_t[k] for k in range(rows_t.shape[0])], axis=1)
        sums = dot(left_side, jnp.concatenate([slab[b1], slab[b2]], axis=1))
        for b, part in ((b1, sums[:, :tile]), (b2, sums[:, tile:])):
            totals[b] = part
            totals_low[b] = part.astype(BF16)

    ways = (("m", -1, down, 0), ("p", 1, up, 1))

    def leaf(name, h, p, d, device, one=False):
        at = pl.ds(h * middle, middle)
        src, dst = totals_low.at[block(p, d), at], land_r.at[PIECES[name], at]
        send(f"r{name}" if one else f"r{name}{h}", src, dst, device)

    def join(name, children, h, p, d, device):
        at, slot = pl.ds(h * middle, middle), PIECES[name]
        value = totals[block(p, d), at]
        for child in children:
            arrived(f"r{child}" if child[1:] in ("w4", "o4") else f"r{child}{h}")
            value = value + land_r[PIECES[child], at].astype(F32)
        stage_r[slot, at] = value.astype(BF16)
        send(f"r{name}{h}", stage_r.at[slot, at], land_r.at[slot, at], device)

    column_sums(block(0, 4), block(1, 4))
    for way, s, device, e in ways:
        leaf(way + "o4", e, 1, 4, device, one=True)
    for way, s, device, e in ways:
        leaf(way + "w4", e, 0, 4, device, one=True)
    column_sums(block(1, 3), block(1, -3))
    for way, s, device, e in ways:
        leaf(way + "o3", 1 - e, 1, 3 * s, device)
    column_sums(block(0, 3), block(0, -3))
    for way, s, device, e in ways:
        leaf(way + "w3", 1 - e, 0, 3 * s, device)
    column_sums(block(1, 2), block(1, -2))
    column_sums(block(1, 0), own)
    for h in (0, 1):
        leaf("y0", h, 1, 0, over)
    for way, s, device, e in ways:
        join(way + "o3", [way + "o4"], e, 1, 3 * s, device)
    for way, s, device, e in ways:
        join(way + "w3", [way + "w4"], e, 0, 3 * s, device)
    for way, s, device, e in ways:
        join(way + "o2", [way + "o3"], 1 - e, 1, 2 * s, device)
    column_sums(block(1, 1), block(1, -1))
    column_sums(block(0, 2), block(0, -2))
    for way, s, device, e in ways:
        join(way + "o2", [way + "o3"], e, 1, 2 * s, device)
    for way, s, device, e in ways:
        join(way + "w2", [way + "w3"], 1 - e, 0, 2 * s, device)
    column_sums(block(0, 1), block(0, -1))
    for way, s, device, e in ways:
        join(way + "y1", [way + "o2"], 1 - e, 1, s, over)
    for way, s, device, e in ways:
        join(way + "w2", [way + "w3"], e, 0, 2 * s, device)
    for way, s, device, e in ways:
        join(way + "y1", [way + "o2"], e, 1, s, over)

    blocks = range(panel.shape[0])
    slim = width // 16
    grad_low = pre_grad_t.astype(BF16)
    for i in range(width // tile):
        columns = slice(i * tile, (i + 1) * tile)
        term = dot(
            jnp.concatenate([totals_low[b] for b in blocks] + [grad_low], axis=1),
            jnp.concatenate(
                [panel[b, :, columns] for b in blocks] + [panel[own][:, columns]], axis=0
            ),
        ).T
        wown[columns] = term
        for j in range(tile // slim):
            wsend[i * (tile // slim) + j] = term[j * slim : (j + 1) * slim].astype(BF16)
    wcopies = []
    for i in range(1, 16):
        to = lax.rem(c + i, 16)
        copy = pltpu.make_async_remote_copy(
            wsend.at[to], wland.at[i], wsend_sem.at[i], wrecv_sem.at[i], device_id=(to, r)
        )
        copy.start()
        wcopies.append(copy)
    for way, s, device, e in ways:
        join(way + "w1", [way + "w2", way + "y1"], 1 - e, 0, s, device)
    total = wown[pl.ds(pl.multiple_of(c * slim, slim), slim)]
    for i, copy in enumerate(wcopies):
        copy.wait_recv()
        total = total + wland[i + 1].astype(F32)
    two, lanes = slim // 16, tile
    for i in range(16):
        rows = total[i * two : (i + 1) * two]
        wsend2[i] = jnp.concatenate(
            [rows[:, q * lanes : (q + 1) * lanes] for q in range(width // lanes)], axis=0
        )
    wcopies2 = []
    for i in range(1, 16):
        to = lax.rem(r + i, 16)
        copy = pltpu.make_async_remote_copy(
            wsend2.at[to], wland2.at[i], wsend_sem.at[16 + i], wrecv_sem.at[16 + i],
            device_id=(c, to),
        )
        copy.start()
        wcopies2.append(copy)
    for way, s, device, e in ways:
        join(way + "w1", [way + "w2", way + "y1"], e, 0, s, device)

    back = []
    for h in (0, 1):
        at = pl.ds(h * middle, middle)
        value = totals[own, at] + pre_grad_t[h * middle : (h + 1) * middle]
        for name in ("y0", "mw1", "pw1"):
            arrived(f"r{name}{h}")
            value = value + land_r[PIECES[name], at].astype(F32)
        back.append(value)
    back = jnp.concatenate(back, axis=0).T.astype(BF16)
    input_rows = lax.dot_general(
        back, w_ref[...], (((1,), (1,)), ((), ())), preferred_element_type=F32
    ).astype(BF16)
    fgrad_ref[...] = dot(place.astype(BF16), input_rows).astype(BF16)

    pair = wsend2[r]
    for i, copy in enumerate(wcopies2):
        copy.wait_recv()
        pair = pair + wland2[i + 1]
    pair = jnp.concatenate([pair[q * two : (q + 1) * two] for q in range(width // lanes)], axis=1)
    wgrad_ref[...] = pair * (1.0 / math.sqrt(tile * 256))
    for copy in [*copies.values(), *wcopies, *wcopies2]:
        copy.wait_send()


def on_device(features, reorder, weight, adjacency, tile_block, live_counts, grad_out):
    tile, width = features.shape
    _, _, rows, slots, _, _ = adjacency.shape
    blocks = 16
    vmem = pl.BlockSpec(memory_space=pltpu.VMEM)
    return pl.pallas_call(
        layer_kernel,
        in_specs=[
            vmem, vmem, vmem, pl.BlockSpec(memory_space=pl.ANY), vmem,
            pl.BlockSpec(memory_space=pltpu.SMEM), vmem,
        ],
        out_specs=[vmem, vmem, vmem],
        out_shape=[
            jax.ShapeDtypeStruct((tile, width), BF16),
            jax.ShapeDtypeStruct((width // 256, width), F32),
            jax.ShapeDtypeStruct((tile, width), BF16),
        ],
        scratch_shapes=[
            pltpu.VMEM((rows, slots, tile, tile), BF16),
            pltpu.VMEM((blocks, rows * tile, tile), BF16),
            pltpu.VMEM((rows, slots * 16), F32),
            pltpu.VMEM((rows, 8, tile), F32),
            pltpu.VMEM((blocks, tile, width), BF16),
            pltpu.VMEM((blocks, tile, width), BF16),
            pltpu.VMEM((rows * tile, width), F32),
            pltpu.VMEM((len(SLOTS), tile + 16, width), BF16),
            pltpu.VMEM((len(SLOTS), tile + 16, width), BF16),
            pltpu.VMEM((16, width, tile), BF16),
            pltpu.VMEM((16, width, tile), F32),
            pltpu.VMEM((16, width, tile), BF16),
            pltpu.VMEM((len(PIECES), width, tile), BF16),
            pltpu.VMEM((len(PIECES), width, tile), BF16),
            pltpu.VMEM((16, width // 16, width), BF16),
            pltpu.VMEM((16, width // 16, width), BF16),
            pltpu.VMEM((width, width), F32),
            pltpu.VMEM((16, 8, tile), F32),
            pltpu.VMEM((16, 8, tile), F32),
            pltpu.SemaphoreType.DMA((rows,)),
            pltpu.SemaphoreType.DMA((N_SEMS,)),
            pltpu.SemaphoreType.DMA((N_SEMS,)),
            pltpu.SemaphoreType.DMA((32,)),
            pltpu.SemaphoreType.DMA((32,)),
        ],
        compiler_params=pltpu.CompilerParams(
            collective_id=0, has_side_effects=True, vmem_limit_bytes=60 * 2**20
        ),
    )(features, reorder, weight, adjacency, tile_block, live_counts, grad_out)


def solution(mesh):
    nodes = P(("col", "rep"), None)
    return jax.shard_map(
        on_device,
        mesh=mesh,
        in_specs=(
            nodes,
            nodes,
            P(),
            P("col", "rep", None, None, None, None),
            P("col", "rep", None, None),
            P("col", "rep", None),
            nodes,
        ),
        out_specs=(nodes, nodes, nodes),
        check_vma=False,
    )
```

time: 133 us -> 104 us (0.78)
  Pallas kernels: 128 us -> 98.7 us
    pallas_call x1 -> x0, Pallas kernels: 14.5 us -> none  [dense_slab(): pl.pallas_call(slab_kernel, grid_spec=pltpu.PrefetchScalarGridSpec(num_sc...]
    pallas_call x1, Pallas kernels: 113 us -> 98.7 us  [on_device(): pl.pallas_call(layer_kernel, in_specs=[vmem, vmem, vmem, pl.BlockSpec(mem...]
where the time goes in v2:
time: 104 us
  Pallas kernels  98.7 us (95%)
  local copies, waits for them, and re-layouts  4.41 us (4%)
    pallas_call x1, Pallas kernels, on_device(): pl.pallas_call(layer_kernel, in_specs=[vmem, vmem, vmem, pl.BlockSpec(mem...  98.7 us
    unnamed x3, local copies, waits for them, and re-layouts  4.41 us

profile of v2, /device:TPU:1, one launch (start us, length us, event | category | flops | bytes accessed | tf_op | source)
XLA Modules:
  0.0 103.8 jit_solution(5623986453000258309)
XLA Ops:
  0.6 98.7 %shard_map.94 = (bf16[128,512]{1,0:T(8,128)(2,1)}, f32[2,512]{1,0:T(2,128)}, bf16[128,512]{1,0:T(8,128)(2,1)}) custom-call(bf16[128,512]{1,0:T(8,128)(2,1)} %feat_ref.1, s32[1,128]{1,0:T(1,128)} %order_ref.1, bf16[512,512]{1,0:T(8,128)(2,1)} %w_ref.1, bf16[1,1,16,16,128,128]{5,4,3,2,1,0:T(8,128)(2,1)} %tiles_hbm.1, s32[1,1,16,16]{3,2,1,0:T(8,128)} %block_ref.1, ...), custom_call_target="tpu_custom_call" | custom-call | tf_op jit(solution)/shard_map/pallas_call | solution.py:448
  99.4 1.6 %copy.13 = bf16[128,512]{1,0:T(8,128)(2,1)} copy(bf16[128,512]{1,0:T(8,128)(2,1)} %get-tuple-element.6) | data formatting | bytes 262144
  100.9 1.3 %copy.14 = f32[2,512]{1,0:T(2,128)} copy(f32[2,512]{1,0:T(2,128)} %get-tuple-element.7) | data formatting | bytes 8192
  102.2 1.6 %copy.15 = bf16[128,512]{1,0:T(8,128)(2,1)} copy(bf16[128,512]{1,0:T(8,128)(2,1)} %get-tuple-element.8) | data formatting | bytes 262144

commit v3 on v2

--- a/solution.py
+++ b/solution.py
@@ -37,7 +37,8 @@
     feat_ref, order_ref, w_ref, tiles_hbm, block_ref, count_ref, grad_ref,
     act_ref, wgrad_ref, fgrad_ref,
     tiles, slab, ids, degrees, panel, projected, acc, stage_f, land_f, rows_t, totals, totals_low,
-    stage_r, land_r, wsend, wland, wown, wsend2, wland2,
+    stage_r, land_r, wown, wcore, wcore_in, wmid, wmid_low, wmid_in, wlast, wlast_low, wlast_in,
+    wsend2, wland2,
     tile_sem, send_sem, recv_sem, wsend_sem, wrecv_sem,
 ):
     tile, width = feat_ref.shape
@@ -346,33 +347,36 @@
     column_sums(block(0, 3), block(0, -3))
     for way, s, device, e in ways:
         leaf(way + "w3", 1 - e, 0, 3 * s, device)
+    column_sums(block(1, 0), own)
+    for h in (0, 1):
+        leaf("y0", h, 1, 0, over)
     column_sums(block(1, 2), block(1, -2))
-    column_sums(block(1, 0), own)
-    for h in (0, 1):
-        leaf("y0", h, 1, 0, over)
     for way, s, device, e in ways:
         join(way + "o3", [way + "o4"], e, 1, 3 * s, device)
     for way, s, device, e in ways:
         join(way + "w3", [way + "w4"], e, 0, 3 * s, device)
+    column_sums(block(1, 1), block(1, -1))
     for way, s, device, e in ways:
         join(way + "o2", [way + "o3"], 1 - e, 1, 2 * s, device)
-    column_sums(block(1, 1), block(1, -1))
     column_sums(block(0, 2), block(0, -2))
+    column_sums(block(0, 1), block(0, -1))
     for way, s, device, e in ways:
         join(way + "o2", [way + "o3"], e, 1, 2 * s, device)
     for way, s, device, e in ways:
         join(way + "w2", [way + "w3"], 1 - e, 0, 2 * s, device)
-    column_sums(block(0, 1), block(0, -1))
-    for way, s, device, e in ways:
-        join(way + "y1", [way + "o2"], 1 - e, 1, s, over)
-    for way, s, device, e in ways:
-        join(way + "w2", [way + "w3"], e, 0, 2 * s, device)
-    for way, s, device, e in ways:
-        join(way + "y1", [way + "o2"], e, 1, s, over)
 
     blocks = range(panel.shape[0])
     slim = width // 16
     grad_low = pre_grad_t.astype(BF16)
+    wcopies = {}
+
+    def wsend(name, i, src, dst, device):
+        copy = pltpu.make_async_remote_copy(
+            src, dst, wsend_sem.at[i], wrecv_sem.at[i], device_id=device
+        )
+        copy.start()
+        wcopies[name] = copy
+
     for i in range(width // tile):
         columns = slice(i * tile, (i + 1) * tile)
         term = dot(
@@ -383,36 +387,47 @@
         ).T
         wown[columns] = term
         for j in range(tile // slim):
-            wsend[i * (tile // slim) + j] = term[j * slim : (j + 1) * slim].astype(BF16)
-    wcopies = []
-    for i in range(1, 16):
-        to = lax.rem(c + i, 16)
-        copy = pltpu.make_async_remote_copy(
-            wsend.at[to], wland.at[i], wsend_sem.at[i], wrecv_sem.at[i], device_id=(to, r)
-        )
-        copy.start()
-        wcopies.append(copy)
+            rows = term[j * slim : (j + 1) * slim].astype(BF16)
+            wcore[j % 2, pl.ds((i * 2 + j // 2) * slim, slim)] = rows
+    wsend("core", 0, wcore.at[1 - core], wcore_in, partner)
+
+    for way, s, device, e in ways:
+        join(way + "y1", [way + "o2"], 1 - e, 1, s, over)
+    wcopies["core"].wait_recv()
+    for i in range(4):
+        for j in range(2):
+            at = pl.ds((i * 2 + j) * slim, slim)
+            rows = wown[pl.ds(pl.multiple_of((i * 4 + j * 2 + core) * slim, slim), slim)]
+            rows = rows + wcore_in[at].astype(F32)
+            wmid[i, pl.ds(j * slim, slim)] = rows
+            wmid_low[i, pl.ds(j * slim, slim)] = rows.astype(BF16)
+    for i in range(1, 4):
+        wsend(f"x{i}", i, wmid_low.at[(x + i) % 4], wmid_in.at[i], (group(i, 0, 0), r))
+    for way, s, device, e in ways:
+        join(way + "w2", [way + "w3"], e, 0, 2 * s, device)
+    for way, s, device, e in ways:
+        join(way + "y1", [way + "o2"], e, 1, s, over)
+    pair = wmid[x]
+    for i in range(1, 4):
+        wcopies[f"x{i}"].wait_recv()
+        pair = pair + wmid_in[i].astype(F32)
+    for j in range(2):
+        wlast[j] = pair[j * slim : (j + 1) * slim]
+        wlast_low[j] = pair[j * slim : (j + 1) * slim].astype(BF16)
+    wsend("y", 4, wlast_low.at[1 - yl], wlast_in, beside)
     for way, s, device, e in ways:
         join(way + "w1", [way + "w2", way + "y1"], 1 - e, 0, s, device)
-    total = wown[pl.ds(pl.multiple_of(c * slim, slim), slim)]
-    for i, copy in enumerate(wcopies):
-        copy.wait_recv()
-        total = total + wland[i + 1].astype(F32)
+    wcopies["y"].wait_recv()
+    total = wlast[yl] + wlast_in[...].astype(F32)
     two, lanes = slim // 16, tile
     for i in range(16):
         rows = total[i * two : (i + 1) * two]
         wsend2[i] = jnp.concatenate(
             [rows[:, q * lanes : (q + 1) * lanes] for q in range(width // lanes)], axis=0
         )
-    wcopies2 = []
     for i in range(1, 16):
         to = lax.rem(r + i, 16)
-        copy = pltpu.make_async_remote_copy(
-            wsend2.at[to], wland2.at[i], wsend_sem.at[16 + i], wrecv_sem.at[16 + i],
-            device_id=(c, to),
-        )
-        copy.start()
-        wcopies2.append(copy)
+        wsend(f"r{i}", 16 + i, wsend2.at[to], wland2.at[i], (c, to))
     for way, s, device, e in ways:
         join(way + "w1", [way + "w2", way + "y1"], e, 0, s, device)
 
@@ -431,13 +446,18 @@
     fgrad_ref[...] = dot(place.astype(BF16), input_rows).astype(BF16)
 
     pair = wsend2[r]
-    for i, copy in enumerate(wcopies2):
-        copy.wait_recv()
-        pair = pair + wland2[i + 1]
+    for i in range(1, 16):
+        wcopies[f"r{i}"].wait_recv()
+        pair = pair + wland2[i]
     pair = jnp.concatenate([pair[q * two : (q + 1) * two] for q in range(width // lanes)], axis=1)
     wgrad_ref[...] = pair * (1.0 / math.sqrt(tile * 256))
-    for copy in [*copies.values(), *wcopies, *wcopies2]:
+    for copy in [*copies.values(), *wcopies.values()]:
         copy.wait_send()
+
+
+def place_kernel(*refs):
+    for src, dst in zip(refs[: len(refs) // 2], refs[len(refs) // 2 :], strict=True):
+        dst[...] = src[...]
 
 
 def on_device(features, reorder, weight, adjacency, tile_block, live_counts, grad_out):
@@ -445,7 +465,7 @@
     _, _, rows, slots, _, _ = adjacency.shape
     blocks = 16
     vmem = pl.BlockSpec(memory_space=pltpu.VMEM)
-    return pl.pallas_call(
+    results = pl.pallas_call(
         layer_kernel,
         in_specs=[
             vmem, vmem, vmem, pl.BlockSpec(memory_space=pl.ANY), vmem,
@@ -472,9 +492,15 @@
             pltpu.VMEM((16, width, tile), BF16),
             pltpu.VMEM((len(PIECES), width, tile), BF16),
             pltpu.VMEM((len(PIECES), width, tile), BF16),
-            pltpu.VMEM((16, width // 16, width), BF16),
-            pltpu.VMEM((16, width // 16, width), BF16),
             pltpu.VMEM((width, width), F32),
+            pltpu.VMEM((2, width // 2, width), BF16),
+            pltpu.VMEM((width // 2, width), BF16),
+            pltpu.VMEM((4, width // 8, width), F32),
+            pltpu.VMEM((4, width // 8, width), BF16),
+            pltpu.VMEM((4, width // 8, width), BF16),
+            pltpu.VMEM((2, width // 16, width), F32),
+            pltpu.VMEM((2, width // 16, width), BF16),
+            pltpu.VMEM((width // 16, width), BF16),
             pltpu.VMEM((16, 8, tile), F32),
             pltpu.VMEM((16, 8, tile), F32),
             pltpu.SemaphoreType.DMA((rows,)),
@@ -487,6 +513,12 @@
             collective_id=0, has_side_effects=True, vmem_limit_bytes=60 * 2**20
         ),
     )(features, reorder, weight, adjacency, tile_block, live_counts, grad_out)
+    return pl.pallas_call(
+        place_kernel,
+        in_specs=[vmem] * 3,
+        out_specs=[vmem] * 3,
+        out_shape=[jax.ShapeDtypeStruct(a.shape, a.dtype) for a in results],
+    )(*results)
 
 
 def solution(mesh):

time: 104 us -> 96.8 us (0.931)
  local copies, waits for them, and re-layouts: 4.41 us -> 0 us
  Pallas kernels: 98.7 us -> 95.7 us
    pallas_call x1, Pallas kernels: 98.7 us -> 94 us  [on_device(): pl.pallas_call(layer_kernel, in_specs=[vmem, vmem, vmem, pl.BlockSpec(mem...]
    unnamed x3 -> x0, local copies, waits for them, and re-layouts: 4.41 us -> none
    pallas_call x0 -> x1, Pallas kernels: none -> 1.68 us  [on_device(): pl.pallas_call(place_kernel, in_specs=[vmem] * 3, out_specs=[vmem] * 3, o...]
where the time goes in v3:
time: 96.8 us; the launch traced here: 96.3 us
  Pallas kernels  95.7 us (99%)
    pallas_call x1, Pallas kernels, on_device(): pl.pallas_call(layer_kernel, in_specs=[vmem, vmem, vmem, pl.BlockSpec(mem...  94 us

profile of v3, /device:TPU:1, one launch (start us, length us, event | category | flops | bytes accessed | tf_op | source)
XLA Modules:
  0.0 96.3 jit_solution(12540407476151328762)
XLA Ops:
  0.6 94.0 %shard_map.94 = (bf16[128,512]{1,0:T(8,128)(2,1)}, f32[2,512]{1,0:T(2,128)}, bf16[128,512]{1,0:T(8,128)(2,1)}) custom-call(bf16[128,512]{1,0:T(8,128)(2,1)} %feat_ref.1, s32[1,128]{1,0:T(1,128)} %order_ref.1, bf16[512,512]{1,0:T(8,128)(2,1)} %w_ref.1, bf16[1,1,16,16,128,128]{5,4,3,2,1,0:T(8,128)(2,1)} %tiles_hbm.1, s32[1,1,16,16]{3,2,1,0:T(8,128)} %block_ref.1, ...), custom_call_target="tpu_custom_call" | custom-call | tf_op jit(solution)/shard_map/pallas_call | solution.py:468
  94.6 1.7 %shard_map.95 = (bf16[128,512]{1,0:T(8,128)(2,1)}, f32[2,512]{1,0:T(2,128)}, bf16[128,512]{1,0:T(8,128)(2,1)}) custom-call(bf16[128,512]{1,0:T(8,128)(2,1)} %get-tuple-element.6.refs_0_, f32[2,512]{1,0:T(2,128)} %get-tuple-element.7.refs_1_, bf16[128,512]{1,0:T(8,128)(2,1)} %get-tuple-element.8.refs_2_), custom_call_target="tpu_custom_call" | custom-call | tf_op jit(solution)/shard_map/pallas_call | solution.py:516

commit v4 on v3

--- a/solution.py
+++ b/solution.py
@@ -391,8 +391,6 @@
             wcore[j % 2, pl.ds((i * 2 + j // 2) * slim, slim)] = rows
     wsend("core", 0, wcore.at[1 - core], wcore_in, partner)
 
-    for way, s, device, e in ways:
-        join(way + "y1", [way + "o2"], 1 - e, 1, s, over)
     wcopies["core"].wait_recv()
     for i in range(4):
         for j in range(2):
@@ -404,6 +402,8 @@
     for i in range(1, 4):
         wsend(f"x{i}", i, wmid_low.at[(x + i) % 4], wmid_in.at[i], (group(i, 0, 0), r))
     for way, s, device, e in ways:
+        join(way + "y1", [way + "o2"], 1 - e, 1, s, over)
+    for way, s, device, e in ways:
         join(way + "w2", [way + "w3"], e, 0, 2 * s, device)
     for way, s, device, e in ways:
         join(way + "y1", [way + "o2"], e, 1, s, over)
@@ -417,6 +417,8 @@
     wsend("y", 4, wlast_low.at[1 - yl], wlast_in, beside)
     for way, s, device, e in ways:
         join(way + "w1", [way + "w2", way + "y1"], 1 - e, 0, s, device)
+    for way, s, device, e in ways:
+        join(way + "w1", [way + "w2", way + "y1"], e, 0, s, device)
     wcopies["y"].wait_recv()
     total = wlast[yl] + wlast_in[...].astype(F32)
     two, lanes = slim // 16, tile
@@ -428,8 +430,6 @@
     for i in range(1, 16):
         to = lax.rem(r + i, 16)
         wsend(f"r{i}", 16 + i, wsend2.at[to], wland2.at[i], (c, to))
-    for way, s, device, e in ways:
-        join(way + "w1", [way + "w2", way + "y1"], e, 0, s, device)
 
     back = []
     for h in (0, 1):

time: 96.8 us -> 98 us (1.012)
  no operation moved by 1% of the time
where the time goes in v4:
time: 98 us; the launch traced here: 96.8 us
  Pallas kernels  96.2 us (98%)
    pallas_call x1, Pallas kernels, on_device(): pl.pallas_call(layer_kernel, in_specs=[vmem, vmem, vmem, pl.BlockSpec(mem...  94.5 us

profile of v4, /device:TPU:1, one launch (start us, length us, event | category | flops | bytes accessed | tf_op | source)
XLA Modules:
  0.0 96.8 jit_solution(12468853112526240325)
XLA Ops:
  0.6 94.5 %shard_map.94 = (bf16[128,512]{1,0:T(8,128)(2,1)}, f32[2,512]{1,0:T(2,128)}, bf16[128,512]{1,0:T(8,128)(2,1)}) custom-call(bf16[128,512]{1,0:T(8,128)(2,1)} %feat_ref.1, s32[1,128]{1,0:T(1,128)} %order_ref.1, bf16[512,512]{1,0:T(8,128)(2,1)} %w_ref.1, bf16[1,1,16,16,128,128]{5,4,3,2,1,0:T(8,128)(2,1)} %tiles_hbm.1, s32[1,1,16,16]{3,2,1,0:T(8,128)} %block_ref.1, ...), custom_call_target="tpu_custom_call" | custom-call | tf_op jit(solution)/shard_map/pallas_call | solution.py:468
  95.1 1.7 %shard_map.95 = (bf16[128,512]{1,0:T(8,128)(2,1)}, f32[2,512]{1,0:T(2,128)}, bf16[128,512]{1,0:T(8,128)(2,1)}) custom-call(bf16[128,512]{1,0:T(8,128)(2,1)} %get-tuple-element.6.refs_0_, f32[2,512]{1,0:T(2,128)} %get-tuple-element.7.refs_1_, bf16[128,512]{1,0:T(8,128)(2,1)} %get-tuple-element.8.refs_2_), custom_call_target="tpu_custom_call" | custom-call | tf_op jit(solution)/shard_map/pallas_call | solution.py:516
